TPU v7x, 128 devices: a whole 4x4x4 slice. The times are simulated.
128 devices in a mesh: seq: 32 (over z, x_lo, y), head: 4 (over x_hi, core).
Axes of the slice: x: 4 (x_hi: 2, x_lo: 2; x = x_hi * 2 + x_lo), y: 4, z: 4, core: 2. Of those that a mesh axis runs over, the one named last changes fastest.
Arguments:
- queries: bfloat16 [2, 4096, 3584], P(None, 'seq', 'head')
- fine_keys: bfloat16 [2, 4096, 3584], P(None, 'seq', 'head')
- fine_values: bfloat16 [2, 4096, 3584], P(None, 'seq', 'head'), may hold values from -48 to 48
- cache_keys: bfloat16 [2, 1024, 3584], P(None, ('seq', 'head')), may hold values from -6 to 6
- cache_values: bfloat16 [2, 1024, 3584], P(None, ('seq', 'head')), may hold values from -48 to 48
- prefix_len: int32 [2], replicated, may hold values from 512 to 1024, as said below
- out_weight: bfloat16 [3584, 3584], P('head'), may hold values from -0.375 to 0.375
Outputs:
- projected: bfloat16 [2, 4096, 3584], P(None, 'seq', 'head')
Inputs may be any that keep to these rules, and one draw needn't show every extreme that they name: `prefix_len`: the first request sees all 1024 cached tokens.
All inputs are finite; a program needn't handle non-finite values.
Results may differ from a plain program's by a relative error of at most 0.015.
Values may be sent and summed in bfloat16 or wider, within the bound.
A program may use at most 192 MiB of HBM per device.

v0:
```python
import jax
import jax.numpy as jnp
from jax import lax
from jax.sharding import PartitionSpec as P

HD = 128


def per_device(queries, fine_keys, fine_values, cache_keys, cache_values, prefix_len, out_weight):
    req_count, tok_rows, feat_width = queries.shape
    head_count = feat_width // HD
    scale = HD ** (-0.5)
    coarse_keys, coarse_values = (
        lax.all_to_all(cache_keys, "head", split_axis=2, concat_axis=1, tiled=True),
        lax.all_to_all(cache_values, "head", split_axis=2, concat_axis=1, tiled=True),
    )
    query_heads = queries.reshape(req_count, tok_rows, head_count, HD).transpose(0, 2, 1, 3)
    start_carry = (
        jnp.full((req_count, head_count, tok_rows), -1e30, jnp.float32),
        jnp.zeros((req_count, head_count, tok_rows), jnp.float32),
        jnp.zeros((req_count, head_count, tok_rows, HD), jnp.float32),
    )

    def update(carry, key_piece, value_piece, visible):
        run_max, run_sum, run_acc = carry
        key_count = key_piece.shape[1]
        key_heads = key_piece.reshape(req_count, key_count, head_count, HD).transpose(0, 2, 1, 3)
        value_heads = value_piece.reshape(req_count, key_count, head_count, HD).transpose(
            0, 2, 1, 3
        )
        scores = (
            jnp.einsum(
                "rhqd,rhkd->rhqk", query_heads, key_heads, preferred_element_type=jnp.float32
            )
            * scale
        )
        mask_full = visible[:, None, None, :]
        scores = jnp.where(mask_full, scores, jnp.float32(-1e30))
        new_max = jnp.maximum(run_max, jnp.max(scores, axis=3))
        correction = jnp.exp(run_max - new_max)
        weights = jnp.where(mask_full, jnp.exp(scores - new_max[..., None]), jnp.float32(0.0))
        new_sum = run_sum * correction + jnp.sum(weights, axis=3)
        added = jnp.einsum(
            "rhqk,rhkd->rhqd",
            weights.astype(jnp.bfloat16),
            value_heads,
            preferred_element_type=jnp.float32,
        )
        return (new_max, new_sum, run_acc * correction[..., None] + added)

    pieces = (
        lax.all_gather(coarse_keys, "seq", axis=1, tiled=True),
        lax.all_gather(coarse_values, "seq", axis=1, tiled=True),
    )
    key_count = pieces[0].shape[1]
    positions = jnp.arange(key_count, dtype=jnp.int32)
    visible = positions[None, :] < prefix_len[:, None]
    carry = update(start_carry, pieces[0], pieces[1], visible)
    pieces = (
        lax.all_gather(fine_keys, "seq", axis=1, tiled=True),
        lax.all_gather(fine_values, "seq", axis=1, tiled=True),
    )
    visible = jnp.ones((req_count, pieces[0].shape[1]), dtype=bool)
    carry = update(carry, pieces[0], pieces[1], visible)
    run_max, run_sum, run_acc = carry
    attended = (run_acc / run_sum[..., None]).astype(jnp.bfloat16)
    attended = attended.transpose(0, 2, 1, 3).reshape(req_count, tok_rows, feat_width)
    partial_value = jnp.einsum(
        "rtc,cd->rtd", attended, out_weight, preferred_element_type=jnp.float32
    )
    return lax.psum_scatter(
        partial_value.astype(jnp.bfloat16), "head", scatter_dimension=2, tiled=True
    )


def solution(mesh):
    return jax.shard_map(
        per_device,
        mesh=mesh,
        in_specs=(
            P(None, "seq", "head"),
            P(None, "seq", "head"),
            P(None, "seq", "head"),
            P(None, ("seq", "head"), None),
            P(None, ("seq", "head"), None),
            P(),
            P("head", None),
        ),
        out_specs=P(None, "seq", "head"),
        check_vma=False,
    )
```

profile of v0, /device:TPU:1, one launch (start us, length us, event | category | flops | bytes accessed | tf_op | source)
XLA Modules:
  0.0 849.4 jit_solution(6286757233047227155)
XLA Ops:
  6.5 3.8 copy.45
  12.3 10.7 %all_to_all.36 = bf16[4,2,7168]{2,1,0:T(2,128)(2,1)S(1)} all-to-all(bf16[4,2,7168]{2,1,0:T(2,128)(2,1)S(1)} %reshape.74), channel_id=1, replica_groups=mesh['seq'=32,'head'=4] {'head'}, dimensions={0} | all-to-all | bytes 229376 | tf_op jit(solution)/shard_map/all_to_all | solution.py:14
  23.0 2.1 reshape.75
  27.1 2.5 copy.51
  31.6 9.0 %all_to_all.37 = bf16[4,2,7168]{2,1,0:T(2,128)(2,1)S(1)} all-to-all(bf16[4,2,7168]{2,1,0:T(2,128)(2,1)S(1)} %reshape.76), channel_id=1, replica_groups=mesh['seq'=32,'head'=4] {'head'}, dimensions={0} | all-to-all | bytes 229376 | tf_op jit(solution)/shard_map/all_to_all | solution.py:15
  40.5 2.1 reshape.77
  46.6 120.1 %all-gather.5.cloned.1.call-done = bf16[2,1024,896]{2,1,0:T(8,128)(2,1)} async-done(((bf16[2,32,896]{2,1,0:T(8,128)(2,1)}), bf16[2,1024,896]{2,1,0:T(8,128)(2,1)}) %all-gather.5.cloned.1.call-update) | async-done | bytes 3670032 | tf_op jit(solution)/shard_map/all_gather | solution.py:52
  166.7 6.1 copy.48
  172.8 6.0 copy.49
  178.8 143.0 %all-gather.7.cloned.1.call-done = bf16[2,1024,896]{2,1,0:T(8,128)(2,1)} async-done(((bf16[2,32,896]{2,1,0:T(8,128)(2,1)}), bf16[2,1024,896]{2,1,0:T(8,128)(2,1)}) %all-gather.7.cloned.1.call-update) | async-done | bytes 3670032 | tf_op jit(solution)/shard_map/all_gather | solution.py:53
  321.8 6.2 copy.54
  328.0 6.4 fusion.8
  334.4 215.6 %all-gather.9.cloned.1.call-done = bf16[2,4096,896]{1,2,0:T(8,128)(2,1)} async-done(((bf16[2,128,896]{1,2,0:T(8,128)(2,1)}), bf16[2,4096,896]{1,2,0:T(8,128)(2,1)}) %all-gather.9.cloned.1.call-update) | async-done | bytes 14680080 | tf_op jit(solution)/shard_map/all_gather | solution.py:60
  549.9 19.4 %copy.56 = bf16[2,4096,7,128]{3,1,2,0:T(8,128)(2,1)} copy(bf16[2,4096,7,128]{1,3,2,0:T(8,128)(2,1)} %bitcast.90) | data formatting | bytes 29360128 | tf_op jit(solution)/shard_map/reshape | solution.py:27
  569.4 14.9 %multiply_reduce_fusion = (f32[2,7,128]{2,1,0:T(8,128)S(1)}, f32[2,7,128,4096]{3,2,1,0:T(8,128)}) fusion(bf16[2,7,128,128]{2,3,1,0:T(8,128)(2,1)S(1)} %bitcast.101, bf16[2,4096,7,128]{3,1,2,0:T(8,128)(2,1)} %copy.56), kind=kOutput, calls=%fused_computation.1 | convolution fusion | flops 1893726464 | bytes 44506112 | tf_op jit(solution)/shard_map/rhqd,rhkd->rhqk/dot_general | solution.py:32
  584.3 12.6 %fusion = f32[2,7,128]{2,1,0:T(8,128)S(1)} fusion(f32[2,7,128,4096]{3,2,1,0:T(8,128)} %get-tuple-element.13, f32[2,7,128]{2,1,0:T(8,128)S(1)} %get-tuple-element.9), kind=kLoop, calls=%fused_computation.2 | loop fusion | flops 22018304 | bytes 29374464 | tf_op jit(solution)/shard_map/reduce_sum | solution.py:42
  596.9 143.9 %all-gather.11.cloned.1.call-done = bf16[2,4096,896]{2,1,0:T(8,128)(2,1)} async-done(((bf16[2,128,896]{2,1,0:T(8,128)(2,1)}), bf16[2,4096,896]{2,1,0:T(8,128)(2,1)}) %all-gather.11.cloned.1.call-update) | async-done | bytes 14680080 | tf_op jit(solution)/shard_map/all_gather | solution.py:61
  740.8 20.0 %copy.58 = bf16[2,4096,896]{1,2,0:T(8,128)(2,1)} copy(bf16[2,4096,896]{2,1,0:T(8,128)(2,1)} %all-gather.11.cloned.1.call-done) | data formatting | bytes 29360128 | tf_op jit(solution)/shard_map/all_gather | solution.py:61
  760.8 16.1 %fusion.28 = f32[2,128,7,128]{1,3,2,0:T(8,128)S(1)} fusion(bf16[2,7,4096,128]{2,3,1,0:T(8,128)(2,1)} %bitcast.87, f32[2,7,128,4096]{3,2,1,0:T(8,128)} %get-tuple-element.13, f32[2,7,128]{2,1,0:T(8,128)S(1)} %get-tuple-element.9), kind=kOutput, calls=%fused_computation.27 | convolution fusion | flops 1901068288 | bytes 44964864 | tf_op jit(solution)/shard_map/rhqk,rhkd->rhqd/dot_general | solution.py:43
  778.9 2.5 fusion.43
  781.5 2.1 fusion.11
  783.6 3.6 copy.65
  787.2 3.0 copy.71
  790.2 50.2 %reduce-scatter.4.cloned.1.call-done = bf16[896,256]{1,0:T(8,128)(2,1)} async-done(((bf16[3584,256]{1,0:T(8,128)(2,1)}), bf16[896,256]{1,0:T(8,128)(2,1)}) %reduce-scatter.4.cloned.1.call-update) | async-done | bytes 458768
  (44 shorter events, 14.3 us)
Async XLA Ops:
  6.5 20.5 %copy-start.3 = (bf16[2,8,3584]{2,1,0:T(8,128)(2,1)S(1)}, bf16[2,8,3584]{2,1,0:T(8,128)(2,1)}, u32[]{:S(2)}) copy-start(bf16[2,8,3584]{2,1,0:T(8,128)(2,1)} %param.11) | copy-start | bytes 344068
  6.5 160.1 %all-gather.5.cloned.1.call-start = ((), (), s32[]{:S(2)}) async-start(), calls=%async_computation.3 | async-start | bytes 3784704 | tf_op jit(solution)/shard_map/all_gather | solution.py:52
  10.3 34.3 %copy-start.1 = (bf16[2,128,896]{2,1,0:T(8,128)(2,1)S(1)}, bf16[2,128,896]{2,1,0:T(8,128)(2,1)}, u32[]{:S(2)}) copy-start(bf16[2,128,896]{2,1,0:T(8,128)(2,1)} %param.8) | copy-start | bytes 1376260
  12.3 33.9 %copy-start.2 = (bf16[2,128,896]{2,1,0:T(8,128)(2,1)S(1)}, bf16[2,128,896]{2,1,0:T(8,128)(2,1)}, u32[]{:S(2)}) copy-start(bf16[2,128,896]{2,1,0:T(8,128)(2,1)} %param.7) | copy-start | bytes 1376260
  23.0 23.5 %copy-start.4 = (s32[2]{0:T(128)S(1)}, s32[2]{0:T(128)}, u32[]{:S(2)}) copy-start(s32[2]{0:T(128)} %param.12) | copy-start | bytes 28
  27.0 294.8 %all-gather.7.cloned.1.call-start = ((), (), s32[]{:S(2)}) async-start(), calls=%async_computation.4 | async-start | bytes 3784704 | tf_op jit(solution)/shard_map/all_gather | solution.py:53
  44.5 505.4 %all-gather.9.cloned.1.call-start = ((), (), s32[]{:S(2)}) async-start(), calls=%async_computation.5 | async-start | bytes 15138816 | tf_op jit(solution)/shard_map/all_gather | solution.py:60
  45.6 695.2 %all-gather.11.cloned.1.call-start = ((), (), s32[]{:S(2)}) async-start(), calls=%async_computation.6 | async-start | bytes 15138816 | tf_op jit(solution)/shard_map/all_gather | solution.py:61
  46.2 794.2 %reduce-scatter.4.cloned.1.call-start = ((), (), s32[]{:S(2)}) async-start(), calls=%async_computation.7 | async-start | bytes 2293760
  740.8 36.1 %slice-start = ((s8[7340032]{0:T(1024)(128)(4,1)}), s8[3145728]{0:T(1024)(128)(4,1)S(1)}, s32[]{:S(2)}) async-start(s8[7340032]{0:T(1024)(128)(4,1)} %bitcast.88), calls=%async_computation.8 | async-start | bytes 6291456
  760.7 16.1 %slice-start.1 = ((s8[7340032]{0:T(1024)(128)(4,1)}), s8[4194304]{0:T(1024)(128)(4,1)S(1)}, s32[]{:S(2)}) async-start(s8[7340032]{0:T(1024)(128)(4,1)} %bitcast.88), calls=%async_computation.9 | async-start | bytes 8388608
  776.8 2.1 copy-start
  776.9 4.6 slice-start.2
  778.9 2.6 slice-start.3
Sparse Core Ops, SparseCore 0:
  27.1 139.4 all-gather.4
  168.3 153.4 all-gather.6
  323.4 226.4 all-gather.8
  551.4 189.2 all-gather.10
  790.4 50.0 reduce-scatter.3
where the time goes:
time: 851 us; the launch traced here: 849 us
  waiting for transfers between devices  673 us (79%)
  local copies, waits for them, and re-layouts  86.3 us (10%)
  matrix products  42 us (5%)
  blocking collectives  19.6 us (2%)
  other arithmetic  14.7 us (2%)
  between operations  13.4 us (2%)
    all_gather x1, waiting for transfers between devices, per_device(): lax.all_gather(fine_keys, 'seq', axis=1, tiled=True)  216 us
    all_gather x1, waiting for transfers between devices, per_device(): lax.all_gather(fine_values, 'seq', axis=1, tiled=True)  144 us
    all_gather x1, waiting for transfers between devices, per_device(): lax.all_gather(coarse_values, 'seq', axis=1, tiled=True)  143 us
    all_gather x1, waiting for transfers between devices, per_device(): lax.all_gather(coarse_keys, 'seq', axis=1, tiled=True)  120 us
    unnamed x6, waiting for transfers between devices  50.8 us
    reshape x2, local copies, waits for them, and re-layouts, update(): key_piece.reshape(req_count, key_count, head_count, HD)  25.4 us
    unnamed x30, local copies, waits for them, and re-layouts  24.9 us
    dot_general x2, matrix products, update(): jnp.einsum('rhqd,rhkd->rhqk', query_heads, key_heads, preferred_element_t...  21.3 us
  transfers between devices with their start and end apart: 5, of which 5 were waited for; matrix products, arithmetic and copies ran while one was open for 10% of the time, Pallas kernels for 0%

commit v1 on v0

v1 whole, which is shorter than its diff:
```python
import functools

import jax
import jax.numpy as jnp
from jax import lax
from jax.experimental import pallas as pl
from jax.experimental.pallas import tpu as pltpu
from jax.sharding import PartitionSpec as P

MESH = pl.DeviceIdType.MESH
F32, BF = jnp.float32, jnp.bfloat16
HD = 128
HEADS = 7
GW = HEADS * HD
TOK = 128
COARSE = 1024
KEYS = 5120
TQ = 256
CK = 1024
SLOTS = 16
QUART = TOK // 4
PHASES = ((0, 64), (64, 32), (96, 32))
LOG2 = float(HD ** -0.5 * 1.4426950408889634)


def rcopy(src, dst, ssem, rsem, s, g):
    return pltpu.make_async_remote_copy(
        src_ref=src, dst_ref=dst, send_sem=ssem, recv_sem=rsem,
        device_id=(s, g), device_id_type=MESH)


def kernel(q_ref, fk_ref, fv_ref, ck_ref, cv_ref, plen_ref, w_ref, out_ref,
           st1k, st1v, st2k, st2v, kall, vx, kt, qland, sc0, sc1, qx, mx, acc, obuf, att, wv,
           psend, precv, csend,
           st1_ss, st1_rs, k_ss, k_rs, v_ss, v_rs, q_ss, q_rs, fk_ss, fk_rs, fv_ss, fv_rs,
           ck_ss, ck_rs, cv_ss, cv_rs, cf_ss, cf_rs, o_ss, o_rs, p_ss, p_rs, c_ss, c_rs, w_sem):
    s = lax.axis_index("seq")
    g = lax.axis_index("head")
    z, xl, y = s >> 3, (s >> 2) & 1, s & 3
    xh, c = g >> 1, g & 1
    zk = z >> 1
    sib = xh * 2 + 1 - c
    flip = z * 8 + (1 - xl) * 4 + y

    def place(zd, pos):
        return (pos + 8 - 2 * zd) & 7

    def dest(j):
        zb, xb, yb = j >> 3, (j >> 2) & 1, j & 3
        r = (z + zb) & 1
        zd = 2 * c + r
        pos = ((xl + xb) & 1) * 4 + ((y + yb) & 3)
        h = place(zd, pos)
        sd = zd * 8 + pos
        mine = jnp.logical_and(sd == s, zk == c)
        return r, h, sd, mine

    my_r = z & 1
    my_h = place(z, xl * 4 + y)
    active = my_h < HEADS

    def source(j):
        zb, xb, yb = j >> 3, (j >> 2) & 1, j & 3
        zs = 2 * c + ((my_r + zb) & 1)
        return zs, (xl + xb) & 1, (y + 4 - yb) & 3

    barrier = pltpu.get_barrier_semaphore()
    gd = xh * 2 + zk

    def greet(j, carry):
        _, _, sd, mine = dest(j)

        @pl.when(jnp.logical_not(mine))
        def _():
            pl.semaphore_signal(barrier, inc=1, device_id=(sd, gd), device_id_type=MESH)
        return carry
    lax.fori_loop(0, 16, greet, 0)
    for i in range(1, 4):
        pl.semaphore_signal(barrier, inc=1, device_id=(s, (g + i) & 3), device_id_type=MESH)
    for i in range(2):
        pl.semaphore_signal(barrier, inc=1, device_id=(flip, i * 2 + c), device_id_type=MESH)
    wcopy = pltpu.make_async_copy(w_ref, wv, w_sem)
    wcopy.start()
    vx[:, HD:] = jnp.ones((KEYS, HD), BF)
    pl.semaphore_wait(barrier, 21 - jnp.where(zk == c, 1, 0))


    def st1(i, src, dst, n):
        gp = (g + i) & 3
        cols = pl.ds(pl.multiple_of(gp * GW, HD), GW)
        if i == 0:
            return pltpu.make_async_copy(src.at[:, cols], dst.at[g], st1_rs.at[n, 0])
        return rcopy(src.at[:, cols], dst.at[g], st1_ss.at[n, i], st1_rs.at[n, i], s, gp)
    first = [st1(i, src, dst, n) for i in range(4)
             for n, (src, dst) in enumerate(((ck_ref, st1k), (cv_ref, st1v)))]
    for f in first:
        f.start()

    def move(src, dst, ss, rs, sd, mine):
        @pl.when(mine)
        def _():
            pltpu.make_async_copy(src, dst, rs).start()

        @pl.when(jnp.logical_not(mine))
        def _():
            rcopy(src, dst, ss, rs, sd, gd).start()

    has_mine = jnp.logical_and(zk == c, active)

    def sent(piece, n, sem):
        @pl.when(has_mine)
        def _():
            rcopy(piece(n - 1), piece(n - 1), sem, sem, s, sib).wait_send()

        @pl.when(jnp.logical_not(has_mine))
        def _():
            rcopy(piece(n), piece(n), sem, sem, s, sib).wait_send()

    def came(piece, sem):
        rcopy(piece, piece, sem, sem, s, sib).wait_recv()

    def hcols(h):
        return pl.ds(pl.multiple_of(h * HD, HD), HD)

    def krows(slot, n=1):
        return pl.ds(pl.multiple_of(COARSE + slot * TOK, TOK), n * TOK)

    def kv_args(j):
        r, h, sd, mine = dest(j)
        rows = krows(zk * 16 + j)
        return (h, (fk_ref.at[r, :, hcols(h)], kall.at[rows, :], k_ss, k_rs.at[j >> 2], sd, mine),
                (fv_ref.at[r, :, hcols(h)], vx.at[rows, 0:HD], v_ss, v_rs.at[j >> 2], sd, mine))

    def q_args(part):
        rows = pl.ds(0, QUART) if part == 0 else pl.ds(QUART, TOK - QUART)

        def args(j):
            r, h, sd, mine = dest(j)
            return h, (q_ref.at[r, rows, hcols(h)], qland.at[j, rows, :],
                       q_ss.at[part], q_rs.at[part, j >> 3], sd, mine)
        return args

    def c_args(j):
        r, h, sd, mine = dest(j)
        rows = pl.ds(pl.multiple_of(s * 32, 32), 32)
        return (h, (st2k.at[r, :, hcols(h)], kall.at[rows, :], ck_ss, ck_rs, sd, mine),
                (st2v.at[r, :, hcols(h)], vx.at[rows, 0:HD], cv_ss, cv_rs, sd, mine))

    def each(args, what):
        def step(j, carry):
            h, *copies = args(j)

            @pl.when(h < HEADS)
            def _():
                for a in copies:
                    what(*a)
            return carry
        lax.fori_loop(0, 16, step, 0)

    each(kv_args, move)

    for i in range(4):
        for n, (src, dst) in enumerate(((ck_ref, st1k), (cv_ref, st1v))):
            if i == 0:
                st1(0, src, dst, n).wait()
            else:
                st1(i, src, dst, n).wait_recv()
    for r in range(2):
        for a in range(2):
            for src, dst in ((st1k, st2k), (st1v, st2v)):
                lo = src[2 * a].astype(F32)[r * 8:r * 8 + 8]
                hi = src[2 * a + 1].astype(F32)[r * 8:r * 8 + 8]
                dst[r, a * 16:a * 16 + 16, :] = jnp.concatenate([lo, hi], axis=0).astype(BF)
    each(c_args, move)
    each(q_args(0), move)

    ohead = pl.multiple_of(my_h * HD, HD)
    go = xh * 2 + zk

    def o_args(ph, j):
        zs, xs, ys = source(j)
        so = zs * 8 + (1 - xs) * 4 + ys
        rows = pl.ds(*PHASES[ph])
        mine = jnp.logical_and(so == s, zk == c)
        return (obuf.at[j, rows, :], att.at[my_r, rows, pl.ds(ohead, HD)], o_ss.at[ph],
                o_rs.at[ph], so, mine)

    def give_back(ph, first, count):
        def step(j, carry):
            move(*o_args(ph, j))
            return carry
        lax.fori_loop(first, first + count, step, 0)

    def fwd(ref_k, ss, rs, i, owner, is_v):
        rows = krows(owner * 16 + i * 4, 4)
        piece = ref_k.at[rows, 0:HD] if is_v else ref_k.at[rows, :]
        return rcopy(piece, piece, ss.at[i], rs.at[i], s, sib)

    def cfwd(ref_k, n, owner, is_v):
        rows = pl.ds(pl.multiple_of(owner * 512, 512), 512)
        piece = ref_k.at[rows, 0:HD] if is_v else ref_k.at[rows, :]
        return rcopy(piece, piece, cf_ss.at[n], cf_rs.at[n], s, sib)

    def transpose(row):
        for b in range(2):
            rows = pl.ds(pl.multiple_of(row + b * 256, 256), 256)
            kk = kall[rows, :].T
            kt[0:HD, rows] = kk
            kt[HD:, rows] = kk

    @pl.when(active)
    def _():
        def landed(i, carry):
            rows = krows(c * 16 + i * 4, 4)
            came(kall.at[rows, :], k_rs.at[i])
            fwd(kall, fk_ss, fk_rs, i, c, False).start()
            came(vx.at[rows, 0:HD], v_rs.at[i])
            fwd(vx, fv_ss, fv_rs, i, c, True).start()
            return carry
        lax.fori_loop(0, 4, landed, 0)
        rows = pl.ds(pl.multiple_of(c * 512, 512), 512)
        came(kall.at[rows, :], ck_rs)
        cfwd(kall, 0, c, False).start()
        came(vx.at[rows, 0:HD], cv_rs)
        cfwd(vx, 1, c, True).start()

    sent(lambda n: kall.at[0:n * TOK, :], 14, k_ss)
    sent(lambda n: kall.at[0:n * TOK, :], 14, v_ss)
    each(q_args(1), move)

    @pl.when(active)
    def _():
        def mine_t(i, carry):
            transpose(COARSE + c * 2048 + i * 512)
            return carry
        lax.fori_loop(0, 4, mine_t, 0)

        def theirs_t(i, carry):
            fwd(kall, fk_ss, fk_rs, i, 1 - c, False).wait_recv()
            transpose(COARSE + (1 - c) * 2048 + i * 512)
            return carry
        lax.fori_loop(0, 4, theirs_t, 0)

        def theirs_v(i, carry):
            fwd(vx, fv_ss, fv_rs, i, 1 - c, True).wait_recv()
            fwd(kall, fk_ss, fk_rs, i, c, False).wait_send()
            fwd(vx, fv_ss, fv_rs, i, c, True).wait_send()
            return carry
        lax.fori_loop(0, 4, theirs_v, 0)
        cfwd(kall, 0, 1 - c, False).wait_recv()
        cfwd(vx, 1, 1 - c, True).wait_recv()
        cfwd(kall, 0, c, False).wait_send()
        cfwd(vx, 1, c, True).wait_send()

        plen = plen_ref[my_r]
        k0 = kall[COARSE:COARSE + 1, :].astype(F32)
        transpose(0)
        for i in range(2, 4):
            rows = slice(i * 256, (i + 1) * 256)
            seen = (lax.broadcasted_iota(jnp.int32, (256, HD), 0) + i * 256) < plen
            kk = jnp.where(seen, kall[rows, :].astype(F32), k0).astype(BF).T
            kt[0:HD, rows] = kk
            kt[HD:, rows] = kk
            vx[rows, 0:HD] = jnp.where(seen, vx[rows, 0:HD].astype(F32), 0.0).astype(BF)
            vx[rows, HD:] = jnp.where(seen, 1.0, 0.0).astype(BF)

    def part(ph, gp):
        r0, n = PHASES[ph]
        rows = jnp.concatenate([att[0, r0:r0 + n, :], att[1, r0:r0 + n, :]], axis=0)
        cols = pl.ds(pl.multiple_of(gp * GW, HD), GW)
        return jnp.dot(rows, wv[:, cols], preferred_element_type=F32)

    def pcopy(ph, i):
        rows = pl.ds(2 * PHASES[ph][0], 2 * PHASES[ph][1])
        return rcopy(psend.at[i, rows, :], precv.at[i, rows, :], p_ss.at[ph, i], p_rs.at[ph, i], s, sib)

    def ccopy(ph, i, half):
        rows = pl.ds(*PHASES[ph])
        return rcopy(csend.at[i, :, rows, :], out_ref.at[half, :, rows, :], c_ss.at[ph, i],
                     c_rs.at[ph, half], flip, i * 2 + c)

    def give(ph):
        r0, n = PHASES[ph]

        came(att.at[:, pl.ds(r0, n), :], o_rs.at[ph])
        if ph == 0:
            wcopy.wait()

        def step(i, carry):
            psend[i, 2 * r0:2 * (r0 + n), :] = part(ph, i * 2 + 1 - c).astype(BF)
            pcopy(ph, i).start()
            return carry
        lax.fori_loop(0, 2, step, 0)

    def take(ph):
        r0, n = PHASES[ph]

        def step(i, carry):
            val = part(ph, i * 2 + c)
            pcopy(ph, i).wait_recv()
            val = (val + precv[i, 2 * r0:2 * (r0 + n), :].astype(F32)).astype(BF)
            for r in range(2):
                csend[i, r, r0:r0 + n, :] = val[r * n:(r + 1) * n]
            ccopy(ph, i, xh).start()
            return carry
        lax.fori_loop(0, 2, step, 0)

    scs = (sc0, sc1)

    def prep(quart, half):
        slots = pl.ds(half * 8, 8)

        @pl.when(quart == 0)
        def _():
            came(qland.at[slots, pl.ds(0, QUART), :], q_rs.at[0, half])

        @pl.when(quart == 1)
        def _():
            came(qland.at[slots, pl.ds(QUART, TOK - QUART), :], q_rs.at[1, half])
        rows = pl.ds(pl.multiple_of(quart * QUART, QUART), QUART)
        x = qland[half * 8:half * 8 + 8, rows, :].reshape(TQ, HD).astype(F32) * LOG2
        hi = x.astype(BF)
        qx[:, :HD] = hi
        qx[:, HD:] = (x - hi.astype(F32)).astype(BF)
        mx[...] = jnp.full((TQ, HD), -jnp.inf, F32)

    def qk(ci, sc):
        cols = slice(ci * CK, (ci + 1) * CK)
        val = jnp.dot(qx[...], kt[:, cols], preferred_element_type=F32)
        sc[:, cols] = val
        m = mx[...]
        for b in range(CK // HD):
            m = jnp.maximum(m, val[:, b * HD:(b + 1) * HD])
        mx[...] = m

    def pv(ci, sc, mrow):
        cols = slice(ci * CK, (ci + 1) * CK)
        p = jnp.exp2(sc[:, cols] - mrow).astype(BF)
        acc[...] += jnp.dot(p, vx[cols, :], preferred_element_type=F32)

    def tile(quart, half, final=False):
        mrow = jnp.max(mx[...], axis=1, keepdims=True)
        acc[...] = jnp.zeros((TQ, 2 * HD), F32)
        if not final:
            prep(quart + half, 1 - half)
        for ci in range(KEYS // CK):
            if not final:
                qk(ci, scs[1 - half])
            pv(ci, scs[half], mrow)
        o = (acc[:, :HD] / acc[:, HD:]).astype(BF)
        rows = pl.ds(pl.multiple_of(quart * QUART, QUART), QUART)
        obuf[half * 8:half * 8 + 8, rows, :] = o.reshape(8, QUART, HD)

    @pl.when(active)
    def _():
        prep(0, 0)
        for ci in range(KEYS // CK):
            qk(ci, sc0)

    def quarter(quart, carry):
        @pl.when(active)
        def _():
            tile(quart, 0)

            @pl.when(quart == 2)
            def _():
                give_back(1, 0, 8)
            tile(quart, 1)

            @pl.when(quart == 1)
            def _():
                give_back(0, 0, 16)

            @pl.when(quart == 2)
            def _():
                give_back(1, 8, 8)
        return carry
    lax.fori_loop(0, 3, quarter, 0)
    give(0)

    @pl.when(active)
    def _():
        tile(3, 0)
        give_back(2, 0, 8)
    take(0)

    @pl.when(active)
    def _():
        tile(3, 1, True)
        give_back(2, 8, 8)
    give(1)
    take(1)
    for i in range(1, 4):
        for n, (src, dst) in enumerate(((ck_ref, st1k), (cv_ref, st1v))):
            st1(i, src, dst, n).wait_send()
    sent(lambda n: kall.at[0:n * 32, :], 14, ck_ss)
    sent(lambda n: kall.at[0:n * 32, :], 14, cv_ss)
    sent(lambda n: qland.at[0:n, pl.ds(0, QUART), :], 14, q_ss.at[0])
    sent(lambda n: qland.at[0:n, pl.ds(QUART, TOK - QUART), :], 14, q_ss.at[1])
    give(2)
    take(2)

    @pl.when(active)
    def _():
        for ph in range(len(PHASES)):
            sent(lambda n: obuf.at[0:n, pl.ds(*PHASES[ph]), :], 16, o_ss.at[ph])
    for ph in range(len(PHASES)):
        for i in range(2):
            pcopy(ph, i).wait_send()
            ccopy(ph, i, xh).wait_send()
    for ph in range(len(PHASES)):
        for i in range(2):
            ccopy(ph, i, i).wait_recv()


def per_device(queries, fine_keys, fine_values, cache_keys, cache_values, prefix_len, out_weight):
    dma = pltpu.SemaphoreType.DMA
    any_spec = pl.BlockSpec(memory_space=pl.ANY)
    halves = pl.pallas_call(
        kernel,
        out_shape=jax.ShapeDtypeStruct((2, 2, TOK, GW), BF),
        in_specs=[any_spec] * 5 + [pl.BlockSpec(memory_space=pltpu.SMEM), any_spec],
        out_specs=any_spec,
        scratch_shapes=[
            pltpu.VMEM((4, 16, GW), BF), pltpu.VMEM((4, 16, GW), BF),
            pltpu.VMEM((2, 32, GW), BF), pltpu.VMEM((2, 32, GW), BF),
            pltpu.VMEM((KEYS, HD), BF), pltpu.VMEM((KEYS, 2 * HD), BF),
            pltpu.VMEM((2 * HD, KEYS), BF), pltpu.VMEM((SLOTS, TOK, HD), BF),
            pltpu.VMEM((TQ, KEYS), F32), pltpu.VMEM((TQ, KEYS), F32),
            pltpu.VMEM((TQ, 2 * HD), BF), pltpu.VMEM((TQ, HD), F32),
            pltpu.VMEM((TQ, 2 * HD), F32), pltpu.VMEM((SLOTS, TOK, HD), BF),
            pltpu.VMEM((2, TOK, GW), BF), pltpu.VMEM((GW, 4 * GW), BF),
            pltpu.VMEM((2, 2 * TOK, GW), BF), pltpu.VMEM((2, 2 * TOK, GW), BF),
            pltpu.VMEM((2, 2, TOK, GW), BF),
            dma((2, 4)), dma((2, 4)), dma, dma((4,)), dma, dma((4,)),
            dma((2,)), dma((2, 2)), dma((4,)), dma((4,)), dma((4,)), dma((4,)),
            dma, dma, dma, dma, dma((2,)), dma((2,)),
            dma((3,)), dma((3,)), dma((3, 2)), dma((3, 2)), dma((3, 2)), dma((3, 2)), dma,
        ],
        compiler_params=pltpu.CompilerParams(
            collective_id=0, has_side_effects=True, vmem_limit_bytes=58 * 2**20),
        cost_estimate=pl.CostEstimate(flops=7_000_000_000, bytes_accessed=12_000_000, transcendentals=10_000_000),
    )(queries, fine_keys, fine_values, cache_keys.reshape(16, 4 * GW),
      cache_values.reshape(16, 4 * GW), prefix_len, out_weight)
    return (halves[0].astype(F32) + halves[1].astype(F32)).astype(BF)


def solution(mesh):
    return jax.shard_map(
        per_device,
        mesh=mesh,
        in_specs=(
            P(None, "seq", "head"),
            P(None, "seq", "head"),
            P(None, "seq", "head"),
            P(None, ("seq", "head"), None),
            P(None, ("seq", "head"), None),
            P(),
            P("head", None),
        ),
        out_specs=P(None, "seq", "head"),
        check_vma=False,
    )
```

time: 851 us -> 68.7 us (0.08)
  waiting for transfers between devices: 673 us -> 0 us
  local copies, waits for them, and re-layouts: 86.3 us -> 0 us
  Pallas kernels: 0 us -> 66.4 us
  matrix products: 42 us -> 0 us
  blocking collectives: 19.6 us -> 0 us
  between operations: 13.4 us -> 0.01 us
  other arithmetic: 14.7 us -> 2.03 us
    all_gather x4 -> x0, waiting for transfers between devices: 623 us -> none  [the longest x1 216 us: per_device(): lax.all_gather(fine_keys, 'seq', axis=1, tiled=True)]
    pallas_call x0 -> x1, Pallas kernels: none -> 66.4 us  [per_device(): pl.pallas_call(kernel, out_shape=jax.ShapeDtypeStruct((2, 2, TOK, GW), BF...]
    unnamed x6 -> x0, waiting for transfers between devices: 50.8 us -> none
    dot_general x5 -> x0, matrix products: 42 us -> none  [the longest x2 21.3 us: update(): jnp.einsum('rhqd,rhkd->rhqk', query_heads, key_heads, preferred_element_t...]
    all_gather x3 -> x0, local copies, waits for them, and re-layouts: 32.3 us -> none  [the longest x1 20 us: per_device(): lax.all_gather(fine_values, 'seq', axis=1, tiled=True)]
    reshape x2 -> x0, local copies, waits for them, and re-layouts: 25.4 us -> none  [update(): key_piece.reshape(req_count, key_count, head_count, HD)]
    unnamed x30 -> x0, local copies, waits for them, and re-layouts: 24.9 us -> none
    all_to_all x2 -> x0, blocking collectives: 19.6 us -> none  [the longest x1 10.7 us: per_device(): lax.all_to_all(cache_keys, 'head', split_axis=2, concat_axis=1, tiled=True)]
  transfers between devices with their start and end apart: 5 -> 0, of which waited for: 5 -> 0; matrix products, arithmetic and copies ran while one was open for 10% -> 0% of each run, Pallas kernels for 0% -> 0%
where the time goes in v1:
time: 68.7 us; the launch traced here: 68.5 us
  Pallas kernels  66.4 us (97%)
  other arithmetic  2.03 us (3%)
    pallas_call x1, Pallas kernels, per_device(): pl.pallas_call(kernel, out_shape=jax.ShapeDtypeStruct((2, 2, TOK, GW), BF...  66.4 us
    convert_element_type x1, other arithmetic, per_device(): return (halves[0].astype(F32) + halves[1].astype(F32)).astype(BF)  2.03 us

profile of v1, /device:TPU:1, one launch (start us, length us, event | category | flops | bytes accessed | tf_op | source)
XLA Modules:
  0.0 68.5 jit_solution(16886626881259019790)
XLA Ops:
  0.0 66.4 %shard_map.73 = bf16[2,2,128,896]{3,2,1,0:T(8,128)(2,1)} custom-call(bf16[2,128,896]{2,1,0:T(8,128)(2,1)} %q_ref.1, bf16[2,128,896]{2,1,0:T(8,128)(2,1)} %fk_ref.1, bf16[2,128,896]{2,1,0:T(8,128)(2,1)} %fv_ref.1, bf16[16,3584]{1,0:T(8,128)(2,1)} %bitcast.4, bf16[16,3584]{1,0:T(8,128)(2,1)} %bitcast.5, s32[2]{0:T(128)} %plen_ref.1, bf16[896,3584]{1,0:T(8,128)(2,1)} %w_ref.1), custom_call_target="tpu_custom_call" | custom-call | flops 7000000000 | bytes 12000000 | tf_op jit(solution)/shard_map/pallas_call | solution.py:419
  66.5 2.0 %fusion = bf16[2,128,896]{2,1,0:T(8,128)(2,1)} fusion(bf16[2,2,128,896]{3,2,1,0:T(8,128)(2,1)} %shard_map.73), kind=kLoop, calls=%fused_computation.1 | loop fusion | flops 917504 | bytes 1376256 | tf_op jit(solution)/shard_map/convert_element_type | solution.py:445
